TPU v7x, 128 devices: a whole 4x4x4 slice. The times are simulated.
128 devices in a mesh: dom: 32 (over z, x_lo, y), edge: 4 (over x_hi, core).
Axes of the slice: x: 4 (x_hi: 2, x_lo: 2; x = x_hi * 2 + x_lo), y: 4, z: 4, core: 2. Of those that a mesh axis runs over, the one named last changes fastest.
Arguments:
- left_table: float32 [65536, 256], P(('dom', 'edge')), may hold values from -2.4 to 2.4
- left_state: float32 [65536], P(('dom', 'edge')), may hold values from 0.02 to 0.2
- right_table: float32 [65536, 256], P(('dom', 'edge')), may hold values from -2.4 to 2.4
- right_state: float32 [65536], P(('dom', 'edge')), may hold values from 0.02 to 0.2
- relations: float32 [2048, 256], replicated, may hold values from -2.4 to 2.4
- relation_state: float32 [2048], replicated, may hold values from 0.02 to 0.2
- src_rows: int32 [2, 131072], P(None, ('dom', 'edge')), may hold values from 0 to 2047
- dst_rows: int32 [2, 131072], P(None, ('dom', 'edge')), may hold values from 0 to 2047
- rel_ids: int32 [2, 131072], P(None, ('dom', 'edge')), may hold values from 0 to 2047
- neg_rows: int32 [2, 32768], P(None, ('dom', 'edge')), may hold values from 0 to 2047
Outputs:
- left_new: float32 [65536, 256], P(('dom', 'edge'))
- left_state_new: float32 [65536], P(('dom', 'edge'))
- right_new: float32 [65536, 256], P(('dom', 'edge'))
- right_state_new: float32 [65536], P(('dom', 'edge'))
- relations_new: float32 [2048, 256], replicated
- relation_state_new: float32 [2048], replicated
All inputs are finite; a program needn't handle non-finite values.
Results may differ from a plain program's by a relative error of at most 0.0019.
Values may be sent and summed in bfloat16 or wider, within the bound.
A program may use at most 64 MiB of HBM per device.

v0:
```python
import jax
import jax.numpy as jnp
from jax import lax
from jax.sharding import PartitionSpec as P

STEPS = 2


learn_rate = 0.1
neg_weight = 0.0625


def passed_along(value, axis, steps):
    count = lax.axis_size(axis)
    pairs = [(source, (source + steps) % count) for source in range(count)]
    return lax.ppermute(value, axis, pairs)


def adagrad(table, state, grad):
    state = state + jnp.mean(grad * grad, axis=-1)
    return (table - learn_rate * grad / jnp.sqrt(state)[:, None], state)


def spread_rows(matches, values):
    return lax.dot_general(
        matches, values, (((0,), (0,)), ((), ())), preferred_element_type=jnp.float32
    )


def lookup_fold(row_index, portion):
    portion_len = portion.shape[0]
    matches = (row_index[:, None] == jnp.arange(portion_len, dtype=jnp.int32)[None, :]).astype(
        jnp.bfloat16
    )
    return jnp.dot(matches, portion, preferred_element_type=jnp.float32)


def scatter_term(row_index, values, count):
    matches = (row_index[:, None] == jnp.arange(count, dtype=jnp.int32)[None, :]).astype(
        jnp.bfloat16
    )
    return spread_rows(matches, values)


def local(
    left_table,
    left_state,
    right_table,
    right_state,
    relations,
    relation_state,
    src_rows,
    dst_rows,
    rel_ids,
    neg_rows,
):
    quarter = left_table.shape[0]
    width = left_table.shape[1]
    half_dim = width // 2
    edge_count = src_rows.shape[1]
    rel_count = relations.shape[0]
    for bucket in range(STEPS):
        right_table, right_state = passed_along((right_table, right_state), "dom", 1)
        src_index = src_rows[bucket]
        target_index = jnp.concatenate([dst_rows[bucket], neg_rows[bucket]], axis=0)
        left_b = left_table.astype(jnp.bfloat16)
        right_b = right_table.astype(jnp.bfloat16)
        source = lookup_fold(src_index, lax.all_gather(left_b, "edge", axis=0, tiled=True))
        looked = lookup_fold(target_index, lax.all_gather(right_b, "edge", axis=0, tiled=True))
        target = looked[:edge_count]
        negatives_b = looked[edge_count:].astype(jnp.bfloat16)
        rel_matches = (
            rel_ids[bucket][:, None] == jnp.arange(rel_count, dtype=jnp.int32)[None, :]
        ).astype(jnp.bfloat16)
        relation = jnp.dot(
            rel_matches, relations.astype(jnp.bfloat16), preferred_element_type=jnp.float32
        )
        src_re, src_im = (source[:, :half_dim], source[:, half_dim:])
        rel_re, rel_im = (relation[:, :half_dim], relation[:, half_dim:])
        product = jnp.concatenate(
            [src_re * rel_re - src_im * rel_im, src_re * rel_im + src_im * rel_re], axis=-1
        )
        positive = jnp.sum(product * target, axis=-1)
        product_b = product.astype(jnp.bfloat16)
        negative = lax.dot_general(
            product_b, negatives_b, (((1,), (1,)), ((), ())), preferred_element_type=jnp.float32
        )
        grad_pos = -jax.nn.sigmoid(-positive)
        grad_neg = (neg_weight * jax.nn.sigmoid(negative)).astype(jnp.bfloat16)
        grad_q = grad_pos[:, None] * target + jnp.dot(
            grad_neg, negatives_b, preferred_element_type=jnp.float32
        )
        grad_re, grad_im = (grad_q[:, :half_dim], grad_q[:, half_dim:])
        grad_src = jnp.concatenate(
            [grad_re * rel_re + grad_im * rel_im, -grad_re * rel_im + grad_im * rel_re], axis=-1
        ).astype(jnp.bfloat16)
        grad_rel = jnp.concatenate(
            [grad_re * src_re + grad_im * src_im, -grad_re * src_im + grad_im * src_re], axis=-1
        ).astype(jnp.bfloat16)
        grad_dst = (grad_pos[:, None] * product).astype(jnp.bfloat16)
        grad_negrow = spread_rows(grad_neg, product_b).astype(jnp.bfloat16)
        grad_target = jnp.concatenate([grad_dst, grad_negrow], axis=0)
        left_grad = lax.psum_scatter(
            scatter_term(src_index, grad_src, quarter * lax.axis_size("edge")),
            "edge",
            scatter_dimension=0,
            tiled=True,
        )
        right_grad = lax.psum_scatter(
            scatter_term(target_index, grad_target, quarter * lax.axis_size("edge")),
            "edge",
            scatter_dimension=0,
            tiled=True,
        )
        relation_grad = lax.psum(spread_rows(rel_matches, grad_rel), ("dom", "edge"))
        left_table, left_state = adagrad(left_table, left_state, left_grad)
        right_table, right_state = adagrad(right_table, right_state, right_grad)
        relations, relation_state = adagrad(relations, relation_state, relation_grad)
    return (left_table, left_state, right_table, right_state, relations, relation_state)


def solution(mesh):
    placed = (
        P(("dom", "edge"), None),
        P(("dom", "edge")),
        P(("dom", "edge"), None),
        P(("dom", "edge")),
        P(),
        P(),
        P(None, ("dom", "edge")),
        P(None, ("dom", "edge")),
        P(None, ("dom", "edge")),
        P(None, ("dom", "edge")),
    )
    return jax.shard_map(
        local,
        mesh=mesh,
        in_specs=placed,
        out_specs=(
            P(("dom", "edge"), None),
            P(("dom", "edge")),
            P(("dom", "edge"), None),
            P(("dom", "edge")),
            P(),
            P(),
        ),
        check_vma=False,
    )
```

profile of v0, /device:TPU:1, one launch (start us, length us, event | category | flops | bytes accessed | tf_op | source)
XLA Modules:
  0.0 595.4 jit_solution(3652485674751418164)
XLA Ops:
  7.2 1.8 convert_element_type.28
  9.1 2.2 collective-permute-start
  12.1 16.9 %collective-permute-done = f32[512,256]{1,0:T(8,128)S(1)} collective-permute-done((f32[512,256]{1,0:T(8,128)}, f32[512,256]{1,0:T(8,128)S(1)}, u32[]{:S(2)}, u32[]{:S(2)}) %collective-permute-start) | collective-permute-done | bytes 524320 | tf_op jit(solution)/shard_map/ppermute | solution.py:16
  30.7 3.5 fusion.9
  34.7 3.3 fusion.11
  38.2 19.0 %all-gather.7.cloned.1.call-done = bf16[2048,256]{1,0:T(8,128)(2,1)} async-done(((bf16[512,256]{1,0:T(8,128)(2,1)}), bf16[2048,256]{1,0:T(8,128)(2,1)}) %all-gather.7.cloned.1.call-update) | async-done | bytes 1048592 | tf_op jit(solution)/shard_map/all_gather | solution.py:69
  57.1 3.7 fusion.3
  63.8 2.9 fusion.20
  68.1 3.2 fusion.12
  72.2 2.9 fusion.22
  75.2 29.1 %reduce-scatter.5.cloned.1.call-done = f32[512,256]{1,0:T(8,128)} async-done(((f32[2048,256]{1,0:T(8,128)}), f32[512,256]{1,0:T(8,128)}) %reduce-scatter.5.cloned.1.call-update) | async-done | bytes 524304 | tf_op jit(solution)/shard_map/reduce_scatter | solution.py:103
  105.5 1.9 fusion.86
  107.5 1.3 collective-permute-start.1
  108.7 36.6 %reduce-scatter.7.cloned.1.call-done = f32[512,256]{1,0:T(8,128)} async-done(((f32[2048,256]{1,0:T(8,128)}), f32[512,256]{1,0:T(8,128)}) %reduce-scatter.7.cloned.1.call-update) | async-done | bytes 524304 | tf_op jit(solution)/shard_map/reduce_scatter | solution.py:109
  149.1 15.8 %collective-permute-done.2 = f32[512,256]{1,0:T(8,128)S(1)} collective-permute-done((f32[512,256]{1,0:T(8,128)S(1)}, f32[512,256]{1,0:T(8,128)S(1)}, u32[]{:S(2)}, u32[]{:S(2)}) %collective-permute-start.2) | collective-permute-done | bytes 524320 | tf_op jit(solution)/shard_map/ppermute | solution.py:16
  166.5 134.6 %all-reduce.3.cloned.1.call-done = f32[2048,256]{1,0:T(8,128)} async-done(((f32[2048,256]{1,0:T(8,128)}), f32[2048,256]{1,0:T(8,128)}) %all-reduce.3.cloned.1.call-update) | async-done | bytes 2097168 | tf_op jit(solution)/shard_map/psum | solution.py:115
  301.0 2.1 multiply_reduce_fusion.1
  303.3 4.8 fusion.5
  308.0 14.0 %all-gather.9.cloned.1.call-done = bf16[2048,256]{1,0:T(8,128)(2,1)} async-done(((bf16[512,256]{1,0:T(8,128)(2,1)}), bf16[2048,256]{1,0:T(8,128)(2,1)}) %all-gather.9.cloned.1.call-update) | async-done | bytes 1048592 | tf_op jit(solution)/shard_map/all_gather | solution.py:68
  322.1 3.3 fusion.7
  326.6 17.9 %all-gather.11.cloned.1.call-done = bf16[2048,256]{1,0:T(8,128)(2,1)} async-done(((bf16[512,256]{1,0:T(8,128)(2,1)}), bf16[2048,256]{1,0:T(8,128)(2,1)}) %all-gather.11.cloned.1.call-update) | async-done | bytes 1048592 | tf_op jit(solution)/shard_map/all_gather | solution.py:69
  344.5 3.7 fusion.1
  351.6 2.9 fusion.26
  354.5 3.8 fusion.24
  358.7 1.3 convolution_convert_fusion
  360.1 3.3 fusion.14
  364.6 139.4 %all-reduce.5.cloned.1.call-done = f32[2048,256]{1,0:T(8,128)} async-done(((f32[2048,256]{1,0:T(8,128)}), f32[2048,256]{1,0:T(8,128)}) %all-reduce.5.cloned.1.call-update) | async-done | bytes 2097168 | tf_op jit(solution)/shard_map/psum | solution.py:115
  504.0 2.1 multiply_reduce_fusion
  506.7 3.0 divide_subtract_fusion
  509.8 33.6 %reduce-scatter.9.cloned.1.call-done = f32[512,256]{1,0:T(8,128)} async-done(((f32[2048,256]{1,0:T(8,128)}), f32[512,256]{1,0:T(8,128)}) %reduce-scatter.9.cloned.1.call-update) | async-done | bytes 524304 | tf_op jit(solution)/shard_map/reduce_scatter | solution.py:103
  545.2 38.6 %reduce-scatter.11.cloned.1.call-done = f32[512,256]{1,0:T(8,128)} async-done(((f32[2048,256]{1,0:T(8,128)}), f32[512,256]{1,0:T(8,128)}) %reduce-scatter.11.cloned.1.call-update) | async-done | bytes 524304 | tf_op jit(solution)/shard_map/reduce_scatter | solution.py:109
  585.6 2.0 divide_subtract_fusion.2
  (108 shorter events, 26.5 us)
Async XLA Ops:
  7.2 23.4 %copy-start.22 = (s32[2,256]{1,0:T(2,128)S(1)}, s32[2,256]{1,0:T(2,128)}, u32[]{:S(2)}) copy-start(s32[2,256]{1,0:T(2,128)} %param.19) | copy-start | bytes 6148
  7.2 23.4 %copy-start.20 = (s32[2,1024]{1,0:T(2,128)S(1)}, s32[2,1024]{1,0:T(2,128)}, u32[]{:S(2)}) copy-start(s32[2,1024]{1,0:T(2,128)} %param.16) | copy-start | bytes 24580
  7.2 23.5 %copy-start.21 = (s32[2,1024]{1,0:T(2,128)S(1)}, s32[2,1024]{1,0:T(2,128)}, u32[]{:S(2)}) copy-start(s32[2,1024]{1,0:T(2,128)} %param.18) | copy-start | bytes 24580
  7.2 27.5 %all-gather.5.cloned.1.call-start = ((), (), s32[]{:S(2)}) async-start(), calls=%async_computation.4 | async-start | bytes 1310720 | tf_op jit(solution)/shard_map/all_gather | solution.py:68
  9.0 48.1 %all-gather.7.cloned.1.call-start = ((), (), s32[]{:S(2)}) async-start(), calls=%async_computation.5 | async-start | bytes 1310720 | tf_op jit(solution)/shard_map/all_gather | solution.py:69
  9.1 19.9 %collective-permute-start = (f32[512,256]{1,0:T(8,128)}, f32[512,256]{1,0:T(8,128)S(1)}, u32[]{:S(2)}, u32[]{:S(2)}) collective-permute-start(f32[512,256]{1,0:T(8,128)} %param.12), channel_id=1, source_target_pairs={{0,4},{4,8},{8,12},{12,16},{16,20},{20,24},{24,28},{28,32},{32,36}... | collective-permute-start | bytes 1572872 | tf_op jit(solution)/shard_map/ppermute | solution.py:16
  30.5 73.7 %reduce-scatter.5.cloned.1.call-start = ((), (), s32[]{:S(2)}) async-start(), calls=%async_computation.6 | async-start | bytes 2621440 | tf_op jit(solution)/shard_map/reduce_scatter | solution.py:103
  66.7 1.0 copy-start.11
  66.8 78.6 %reduce-scatter.7.cloned.1.call-start = ((), (), s32[]{:S(2)}) async-start(), calls=%async_computation.9 | async-start | bytes 2621440 | tf_op jit(solution)/shard_map/reduce_scatter | solution.py:109
  71.3 229.7 %all-reduce.3.cloned.1.call-start = ((), (), s32[]{:S(2)}) async-start(), calls=%async_computation.8 | async-start | bytes 4194304 | tf_op jit(solution)/shard_map/psum | solution.py:115
  75.1 30.4 %copy-start.19 = (f32[512]{0:T(512)S(1)}, f32[512]{0:T(512)}, u32[]{:S(2)}) copy-start(f32[512]{0:T(512)} %param.11) | copy-start | bytes 6148
  75.1 30.4 %copy-start.2 = (f32[512,256]{1,0:T(8,128)S(1)}, f32[512,256]{1,0:T(8,128)}, u32[]{:S(2)}) copy-start(f32[512,256]{1,0:T(8,128)} %param.10) | copy-start | bytes 1572868
  75.1 32.4 %copy-start.23 = (f32[512]{0:T(512)S(1)}, f32[512]{0:T(512)}, u32[]{:S(2)}) copy-start(f32[512]{0:T(512)} %param.13) | copy-start | bytes 6148
  75.1 71.5 %copy-start.15 = (f32[512,256]{1,0:T(8,128)S(1)}, f32[512,256]{1,0:T(8,128)}, u32[]{:S(2)}) copy-start(f32[512,256]{1,0:T(8,128)} %copy-done.14) | copy-start | bytes 1572868
  75.1 246.9 %all-gather.9.cloned.1.call-start = ((), (), s32[]{:S(2)}) async-start(), calls=%async_computation.7 | async-start | bytes 1310720 | tf_op jit(solution)/shard_map/all_gather | solution.py:68
  107.4 237.1 %all-gather.11.cloned.1.call-start = ((), (), s32[]{:S(2)}) async-start(), calls=%async_computation.10 | async-start | bytes 1310720 | tf_op jit(solution)/shard_map/all_gather | solution.py:69
  107.5 39.1 %collective-permute-start.1 = (f32[512]{0:T(512)S(1)}, f32[512]{0:T(512)S(1)}, u32[]{:S(2)}, u32[]{:S(2)}) collective-permute-start(f32[512]{0:T(512)S(1)} %copy-done.23), channel_id=1, source_target_pairs={{0,4},{4,8},{8,12},{12,16},{16,20},{20,24},{24,28},{28,32},{32,36}... | collective-permute-start | bytes 6152 | tf_op jit(solution)/shard_map/ppermute | solution.py:16
  146.6 156.6 %copy-start.18 = (f32[2048]{0:T(1024)S(1)}, f32[2048]{0:T(1024)}, u32[]{:S(2)}) copy-start(f32[2048]{0:T(1024)} %param.15) | copy-start | bytes 24580
  147.8 17.1 %collective-permute-start.2 = (f32[512,256]{1,0:T(8,128)S(1)}, f32[512,256]{1,0:T(8,128)S(1)}, u32[]{:S(2)}, u32[]{:S(2)}) collective-permute-start(f32[512,256]{1,0:T(8,128)S(1)} %divide_subtract_fusion.4), channel_id=1, source_target_pairs={{0,4},{4,8},{8,12},{12,16},{16,20},{20,24},{24,28},{28,32},{32,36}... | collective-permute-start | bytes 1572872 | tf_op jit(solution)/shard_map/ppermute | solution.py:16
  166.4 337.6 %all-reduce.5.cloned.1.call-start = ((), (), s32[]{:S(2)}) async-start(), calls=%async_computation.13 | async-start | bytes 4194304 | tf_op jit(solution)/shard_map/psum | solution.py:115
  301.0 2.2 copy-start
  322.1 4.4 copy-start.5
  348.5 1.7 copy-start.8
  349.0 1.5 copy-start.6
  354.5 188.9 %reduce-scatter.9.cloned.1.call-start = ((), (), s32[]{:S(2)}) async-start(), calls=%async_computation.11 | async-start | bytes 2621440 | tf_op jit(solution)/shard_map/reduce_scatter | solution.py:103
  358.4 225.4 %reduce-scatter.11.cloned.1.call-start = ((), (), s32[]{:S(2)}) async-start(), calls=%async_computation.12 | async-start | bytes 2621440 | tf_op jit(solution)/shard_map/reduce_scatter | solution.py:109
  363.4 221.6 %collective-permute-start.3 = (f32[512]{0:T(512)S(1)}, f32[512]{0:T(512)S(1)}, u32[]{:S(2)}, u32[]{:S(2)}) collective-permute-start(f32[512]{0:T(512)S(1)} %get-tuple-element.13), channel_id=1, source_target_pairs={{0,4},{4,8},{8,12},{12,16},{16,20},{20,24},{24,28},{28,32},{32,36}... | collective-permute-start | bytes 6152 | tf_op jit(solution)/shard_map/ppermute | solution.py:16
  504.0 2.7 copy-start.1
  506.7 78.9 %copy-start.13 = (f32[512,256]{1,0:T(8,128)S(1)}, f32[512,256]{1,0:T(8,128)}, u32[]{:S(2)}) copy-start(f32[512,256]{1,0:T(8,128)} %copy-done.12) | copy-start | bytes 1572868
  509.8 77.8 %copy-start.3 = (f32[512,256]{1,0:T(8,128)S(1)}, f32[512,256]{1,0:T(8,128)}, u32[]{:S(2)}) copy-start(f32[512,256]{1,0:T(8,128)} %param.10) | copy-start | bytes 1572868
  509.8 77.8 %copy-start.4 = (f32[512,256]{1,0:T(8,128)S(1)}, f32[512,256]{1,0:T(8,128)}, u32[]{:S(2)}) copy-start(f32[512,256]{1,0:T(8,128)} %reduce-scatter.5.cloned.1.call-done) | copy-start | bytes 1572868
  543.3 44.2 %copy-start.16 = (f32[512,256]{1,0:T(8,128)S(1)}, f32[512,256]{1,0:T(8,128)}, u32[]{:S(2)}) copy-start(f32[512,256]{1,0:T(8,128)} %reduce-scatter.9.cloned.1.call-done) | copy-start | bytes 1572868
  (6 other events, 5.1 us)
Sparse Core Ops, SparseCore 0:
  10.3 24.3 all-gather.4
  36.9 20.1 all-gather.6
  66.9 37.3 reduce-scatter.4
  107.5 37.7 reduce-scatter.6
  150.0 150.9 all-reduce.2
  302.6 19.4 all-gather.8
  324.3 20.1 all-gather.10
  354.6 149.3 all-reduce.4
  506.7 36.6 reduce-scatter.8
  546.0 37.7 reduce-scatter.10
where the time goes:
time: 596 us; the launch traced here: 595 us
  waiting for transfers between devices  496 us (83%)
  matrix products  44.6 us (7%)
  other arithmetic  26.4 us (4%)
  between operations  14.6 us (2%)
  local copies, waits for them, and re-layouts  7.01 us (1%)
  starting transfers between devices  6.83 us (1%)
    psum x2, waiting for transfers between devices, local(): lax.psum(spread_rows(rel_matches, grad_rel), ('dom', 'edge'))  274 us
    reduce_scatter x2, waiting for transfers between devices, local(): lax.psum_scatter(scatter_term(target_index, grad_target, quarter * lax.ax...  75.2 us
    reduce_scatter x2, waiting for transfers between devices, local(): lax.psum_scatter(scatter_term(src_index, grad_src, quarter * lax.axis_siz...  62.6 us
    all_gather x2, waiting for transfers between devices, local(): lax.all_gather(right_b, 'edge', axis=0, tiled=True)  36.9 us
    ppermute x4, waiting for transfers between devices, passed_along(): return lax.ppermute(value, axis, pairs)  32.7 us
    dot_general x8, matrix products, spread_rows(): lax.dot_general(matches, values, (((0,), (0,)), ((), ())), preferred_elem...  20.5 us
    all_gather x2, waiting for transfers between devices, local(): lax.all_gather(left_b, 'edge', axis=0, tiled=True)  14.5 us
    dot_general x4, matrix products, lookup_fold(): return jnp.dot(matches, portion, preferred_element_type=jnp.float32)  14.1 us
  transfers between devices with their start and end apart: 14, of which 12 were waited for; matrix products, arithmetic and copies ran while one was open for 8% of the time, Pallas kernels for 0%

commit v1 on v0

v1 whole, which is shorter than its diff:
```python
import functools

import jax
import jax.numpy as jnp
from jax import lax
from jax.experimental import pallas as pl
from jax.experimental.pallas import tpu as pltpu
from jax.sharding import PartitionSpec as P

STEPS = 2
LANES = 128
CHUNK = 256
ROLL_PARTS = 2
MESH = pl.DeviceIdType.MESH
learn_rate = 0.1
neg_weight = 0.0625


def eye(kind=jnp.float32):
    rows = lax.broadcasted_iota(jnp.int32, (LANES, LANES), 0)
    columns = lax.broadcasted_iota(jnp.int32, (LANES, LANES), 1)
    return rows == columns


def to_column(row):
    spread = jnp.where(eye(), jnp.broadcast_to(row, (LANES, LANES)), 0.0)
    return jnp.sum(spread, axis=1, keepdims=True)


def to_row(column):
    spread = jnp.where(eye(), jnp.broadcast_to(column, (LANES, LANES)), 0.0)
    return jnp.sum(spread, axis=0, keepdims=True)


def body(
    n_dom,
    left_in,
    left_state_in,
    right_in,
    right_state_in,
    rel_in,
    rel_state_in,
    src_in,
    dst_in,
    rel_ids_in,
    neg_in,
    left_out,
    left_state_out,
    right_out,
    right_state_out,
    rel_out,
    rel_state_out,
    high_col,
    low_col,
    high_row,
    low_row,
    rel_b,
    source,
    target,
    relation,
    negatives,
    product_b,
    grad_src,
    grad_rel,
    grad_target,
    grad_neg_acc,
    left_all,
    right_all,
    right_own,
    right_table,
    right_state,
    right_next,
    right_state_next,
    left_far_sum,
    left_own_sum,
    right_far_sum,
    right_own_sum,
    rel_own_sum,
    left_to_sib,
    left_from_sib,
    left_to_far,
    left_from_far,
    right_to_sib,
    right_from_sib,
    right_to_far,
    right_from_far,
    rel_to_sib,
    rel_from_sib,
    rel_half,
    rel_parts,
    rel_full,
    send_sems,
    recv_sems,
):
    f32, bf16 = jnp.float32, jnp.bfloat16
    quarter, width = left_in.shape
    edges = src_in.shape[1]
    negs = neg_in.shape[1]
    rels = rel_in.shape[0]
    half_dim = width // 2
    blocks = quarter // LANES
    group = 2 * n_dom
    half_rows = rels // 2
    piece = half_rows // group
    src_at, rel_at, target_at = 0, edges, 2 * edges
    targets = edges + negs

    p = lax.axis_index("dom")
    e = lax.axis_index("edge")
    core = lax.rem(e, 2)
    side = e // 2
    me = p * 2 + side
    sibling = (p, side * 2 + 1 - core)
    far = (p, (1 - side) * 2 + core)
    following = (lax.rem(p + 1, n_dom), e)
    near_quarter = side * 2 + core
    sib_quarter = side * 2 + 1 - core
    far_quarter = (1 - side) * 2 + core
    far_sib_quarter = (1 - side) * 2 + 1 - core

    def peer(k):
        g = lax.rem(me + k, group)
        return (g // 2, lax.rem(g, 2) * 2 + core)

    def rows_of(index, size=quarter):
        return pl.ds(pl.multiple_of(index * size, size), size)

    used = [0]
    sent = []

    def copy(source_ref, target_ref, device):
        index = used[0]
        used[0] += 1
        made = pltpu.make_async_remote_copy(
            src_ref=source_ref,
            dst_ref=target_ref,
            send_sem=send_sems.at[index],
            recv_sem=recv_sems.at[index],
            device_id=device,
            device_id_type=MESH,
        )
        made.start()
        sent.append(made)
        return made

    def each(count, step):
        def run(i, carry):
            step(i)
            return carry

        lax.fori_loop(0, count, run, 0)

    def prepare(t):
        lists = (
            (src_in, src_at, edges),
            (rel_ids_in, rel_at, edges),
            (dst_in, target_at, edges),
            (neg_in, target_at + edges, negs),
        )
        for ref, at, count in lists:

            def block(j, ref=ref, at=at):
                row = ref[t : t + 1, pl.ds(pl.multiple_of(j * LANES, LANES), LANES)]
                place = pl.ds(pl.multiple_of(at + j * LANES, LANES), LANES)
                high = (row >> 7).astype(f32)
                low = (row & 127).astype(f32)
                lanes = lax.broadcasted_iota(jnp.int32, (LANES, LANES), 1).astype(f32)
                subs = lax.broadcasted_iota(jnp.int32, (LANES, LANES), 0).astype(f32)
                low_row[t, :, place] = jnp.where(subs == low, 1.0, 0.0).astype(bf16)
                high_row[t, :, place] = jnp.broadcast_to(high, (16, LANES)).astype(bf16)
                column = jnp.broadcast_to(to_column(row.astype(f32)), (LANES, LANES))
                high_c = jnp.floor(column * (1.0 / LANES))
                low_c = column - LANES * high_c
                high_col[t, place, :] = high_c.astype(bf16)
                low_col[t, place, :] = jnp.where(lanes == low_c, 1.0, 0.0).astype(bf16)

            each(count // LANES, block)

    def level(index, shape):
        return jnp.full(shape, jnp.asarray(index, jnp.int32).astype(f32), f32).astype(bf16)

    def lookup(t, at, count, first_block, n_blocks, table, out, fresh):
        def chunk(i):
            place = pl.ds(pl.multiple_of(at + i * CHUNK, CHUNK), CHUNK)
            high = high_col[t, place, :]
            low = low_col[t, place, :]
            zero = jnp.zeros_like(low)
            matches = jnp.concatenate(
                [
                    jnp.where(high == level(first_block + j, high.shape), low, zero)
                    for j in range(n_blocks)
                ],
                axis=1,
            )
            found = jnp.dot(matches, table[...], preferred_element_type=f32)
            dest = pl.ds(pl.multiple_of(i * CHUNK, CHUNK), CHUNK)
            if fresh:
                out[dest, :] = found
            else:
                out[dest, :] += found

        each(count // CHUNK, chunk)

    def scatter(t, at, count, first_block, n_blocks, values, store):
        def pair(i):
            high = high_row[t, :, at : at + count]
            low = low_row[t, :, at : at + count]
            one, none = jnp.ones_like(high), jnp.zeros_like(high)
            parts = []
            for j in range(2):
                hit = jnp.where(high == level(first_block + 2 * i + j, high.shape), one, none)
                parts.append(low * jnp.concatenate([hit] * (LANES // 16), axis=0))
            matches = jnp.concatenate(parts, axis=0)
            store(
                pl.ds(pl.multiple_of(i * 2 * LANES, 2 * LANES), 2 * LANES),
                jnp.dot(matches, values[...], preferred_element_type=f32),
            )

        each(n_blocks // 2, pair)

    def dense(t):
        negatives[...] = target[edges:, :].astype(bf16)
        grad_neg_acc[...] = jnp.zeros_like(grad_neg_acc)

        def chunk(i):
            place = pl.ds(pl.multiple_of(i * CHUNK, CHUNK), CHUNK)
            s_re, s_im = source[place, :half_dim], source[place, half_dim:]
            r_re, r_im = relation[place, :half_dim], relation[place, half_dim:]
            goal = target[place, :]
            product = jnp.concatenate(
                [s_re * r_re - s_im * r_im, s_re * r_im + s_im * r_re], axis=1
            )
            positive = jnp.sum(product * goal, axis=1, keepdims=True)
            rounded = product.astype(bf16)
            product_b[place, :] = rounded
            n_b = negatives[...]
            negative = lax.dot_general(
                rounded, n_b, (((1,), (1,)), ((), ())), preferred_element_type=f32
            )
            g_pos = -1.0 / (1.0 + jnp.exp(positive))
            g_neg = (neg_weight / (1.0 + jnp.exp(-negative))).astype(bf16)
            g_q = g_pos * goal + jnp.dot(g_neg, n_b, preferred_element_type=f32)
            g_re, g_im = g_q[:, :half_dim], g_q[:, half_dim:]
            grad_src[place, :half_dim] = (g_re * r_re + g_im * r_im).astype(bf16)
            grad_src[place, half_dim:] = (g_im * r_re - g_re * r_im).astype(bf16)
            grad_rel[place, :half_dim] = (g_re * s_re + g_im * s_im).astype(bf16)
            grad_rel[place, half_dim:] = (g_im * s_re - g_re * s_im).astype(bf16)
            grad_target[place, :] = (g_pos * product).astype(bf16)
            grad_neg_acc[...] += lax.dot_general(
                g_neg, rounded, (((0,), (0,)), ((), ())), preferred_element_type=f32
            )

        each(edges // CHUNK, chunk)
        grad_target[edges:, :] = grad_neg_acc[...].astype(bf16)

    def adagrad(table, state, grad_of, table_to, state_to, block):
        place = rows_of(block, LANES)
        grad = grad_of(place)
        column = to_column(state[pl.ds(block, 1), :])
        column = column + jnp.mean(grad * grad, axis=1, keepdims=True)
        table_to[place, :] = table[place, :] - learn_rate * grad / jnp.sqrt(column)
        state_to[pl.ds(block, 1), :] = to_row(column)

    def reduce_begin(t, at, count, values, to_sib, from_sib, far_sum, own_sum):
        copies = []
        for i, quarter_index in enumerate((far_sib_quarter, sib_quarter)):

            def store(place, value, i=i):
                to_sib[t, i, place, :] = value.astype(bf16)

            scatter(t, at, count, quarter_index * blocks, blocks, values, store)
            copies.append(copy(to_sib.at[t, i], from_sib.at[t, i], sibling))
        for quarter_index, total in ((far_quarter, far_sum), (near_quarter, own_sum)):

            def keep(place, value, total=total):
                total[place, :] = value

            scatter(t, at, count, quarter_index * blocks, blocks, values, keep)
        return copies

    def reduce_far(t, copies, from_sib, far_sum, to_far, from_far):
        copies[0].wait_recv()
        to_far[t] = (far_sum[...] + from_sib[t, 0].astype(f32)).astype(bf16)
        return copy(to_far.at[t], from_far.at[t], far)

    def reduce_end(t, copies, far_copy, own_sum, from_sib, from_far):
        copies[1].wait_recv()
        far_copy.wait_recv()

        def grad_of(place):
            return (
                own_sum[place, :]
                + from_sib[t, 1, place, :].astype(f32)
                + from_far[t, place, :].astype(f32)
            )

        return grad_of

    def rel_begin(t):
        pairs = half_rows // LANES

        def store(place, value):
            rel_to_sib[t, place, :] = value.astype(bf16)

        scatter(t, rel_at, edges, (1 - core) * pairs, pairs, grad_rel, store)
        swap = copy(rel_to_sib.at[t], rel_from_sib.at[t], sibling)

        def keep(place, value):
            rel_own_sum[place, :] = value

        scatter(t, rel_at, edges, core * pairs, pairs, grad_rel, keep)
        return swap

    many = pl.ds(0, (group - 1) * piece)

    def take_sems():
        index = used[0]
        used[0] += 1
        return send_sems.at[index], recv_sems.at[index]

    def wait_many(t, sem):
        whole = rel_parts.at[t, many]
        pltpu.make_async_copy(whole, whole, sem).wait()

    def rel_spread(t, swap):
        swap.wait_recv()
        rel_half[t] = (rel_own_sum[...] + rel_from_sib[t].astype(f32)).astype(bf16)
        sems = take_sems()

        def send(k):
            k = k + 1
            g = lax.rem(me + k, group)
            pltpu.make_async_remote_copy(
                src_ref=rel_half.at[t, rows_of(g, piece)],
                dst_ref=rel_parts.at[t, rows_of(k - 1, piece)],
                send_sem=sems[0],
                recv_sem=sems[1],
                device_id=peer(k),
                device_id_type=MESH,
            ).start()

        each(group - 1, send)
        return sems

    def rel_gather(t, sems):
        wait_many(t, sems[1])
        total = rel_half[t, rows_of(me, piece), :].astype(f32)
        for k in range(group - 1):
            total = total + rel_parts[t, k * piece : (k + 1) * piece, :].astype(f32)
        place = rows_of(core * group + me, piece)
        rel_full[t, place, :] = total.astype(bf16)
        more = take_sems()

        def send(k):
            pltpu.make_async_remote_copy(
                src_ref=rel_full.at[t, place],
                dst_ref=rel_full.at[t, place],
                send_sem=more[0],
                recv_sem=more[1],
                device_id=peer(k + 1),
                device_id_type=MESH,
            ).start()

        each(group - 1, send)
        wait_many(t, sems[0])
        return more

    def rel_back(t, more):
        wait_many(t, more[1])
        ours = rows_of(core, half_rows)
        back = copy(rel_full.at[t, ours], rel_full.at[t, ours], sibling)
        wait_many(t, more[0])
        return back

    def rel_update(t, back, table, state):
        back.wait_recv()

        def block(i):
            def grad_of(place):
                return rel_full[t, place, :].astype(f32)

            adagrad(table, state, grad_of, rel_out, rel_state_out, i)

        each(rels // LANES, block)

    def round_relations(table):
        def block(i):
            place = rows_of(i, CHUNK)
            rel_b[place, :] = table[place, :].astype(bf16)

        each(rels // CHUNK, block)

    def left_send(t):
        mine = left_all.at[t, rows_of(near_quarter)]
        return copy(mine, mine, far), copy(mine, mine, sibling)

    def left_forward(t, far_copy):
        far_copy.wait_recv()
        theirs = left_all.at[t, rows_of(far_quarter)]
        return copy(theirs, theirs, sibling)

    part = quarter // ROLL_PARTS

    def part_of(index, i):
        return pl.ds(pl.multiple_of(index * quarter + i * part, part), part)

    def right_send(t):
        return [
            copy(
                right_own.at[t, pl.ds(i * part, part)],
                right_all.at[t, part_of(near_quarter, i)],
                following,
            )
            for i in range(ROLL_PARTS)
        ]

    def right_spread(t, rolled):
        to_far, to_sib = [], []
        for i, made in enumerate(rolled):
            made.wait_recv()
            mine = right_all.at[t, part_of(near_quarter, i)]
            to_far.append(copy(mine, mine, far))
            to_sib.append(copy(mine, mine, sibling))
        return to_far, to_sib

    def right_forward(t, to_far):
        forwarded = []
        for i, made in enumerate(to_far):
            made.wait_recv()
            theirs = right_all.at[t, part_of(far_quarter, i)]
            forwarded.append(copy(theirs, theirs, sibling))
        return forwarded

    def wait_all(copies):
        for made in copies:
            made.wait_recv()

    def look_left(t, index, fresh=False):
        lookup(
            t, src_at, edges, index * blocks, blocks, left_all.at[t, rows_of(index)], source, fresh
        )

    def look_right(t, index, fresh=False):
        lookup(
            t,
            target_at,
            targets,
            index * blocks,
            blocks,
            right_all.at[t, rows_of(index)],
            target,
            fresh,
        )

    def look_relation(t):
        lookup(t, rel_at, edges, 0, rels // LANES, rel_b, relation, True)

    def update(table, state, grad_of, table_to, state_to):
        each(blocks, functools.partial(adagrad, table, state, grad_of, table_to, state_to))

    barrier = pltpu.get_barrier_semaphore()
    pl.semaphore_signal(barrier, inc=1, device_id=sibling, device_id_type=MESH)

    def greet(k):
        pl.semaphore_signal(barrier, inc=1, device_id=peer(k + 1), device_id_type=MESH)

    each(group - 1, greet)
    left_all[0, rows_of(near_quarter), :] = left_in[...].astype(bf16)
    right_own[0] = right_in[...].astype(bf16)
    pl.semaphore_wait(barrier, group)

    rolled = right_send(0)
    left_far, left_sib = left_send(0)
    round_relations(rel_in)
    prepare(0)
    look_relation(0)
    look_left(0, near_quarter, True)
    left_sib.wait_recv()
    look_left(0, sib_quarter)
    right_far, right_sib = right_spread(0, rolled)
    table_roll = copy(right_in, right_table.at[0], following)
    state_roll = copy(right_state_in, right_state.at[0], following)
    left_far_sib = left_forward(0, left_far)
    look_left(0, far_quarter)
    look_right(0, near_quarter, True)
    left_far_sib.wait_recv()
    look_left(0, far_sib_quarter)
    wait_all(right_sib)
    look_right(0, sib_quarter)
    prepare(1)
    right_far_sib = right_forward(0, right_far)
    look_right(0, far_quarter)
    wait_all(right_far_sib)
    look_right(0, far_sib_quarter)
    dense(0)

    right_copies = reduce_begin(
        0, target_at, targets, grad_target, right_to_sib, right_from_sib, right_far_sum, right_own_sum
    )
    right_home = reduce_far(0, right_copies, right_from_sib, right_far_sum, right_to_far, right_from_far)
    swap = rel_begin(0)
    spread = rel_spread(0, swap)
    left_copies = reduce_begin(
        0, src_at, edges, grad_src, left_to_sib, left_from_sib, left_far_sum, left_own_sum
    )
    left_home = reduce_far(0, left_copies, left_from_sib, left_far_sum, left_to_far, left_from_far)
    table_roll.wait_recv()
    state_roll.wait_recv()
    right_grad = reduce_end(0, right_copies, right_home, right_own_sum, right_from_sib, right_from_far)
    update(right_table.at[0], right_state.at[0], right_grad, right_next, right_state_next)
    right_own[1] = right_next[...].astype(bf16)
    rolled = right_send(1)
    gathered = rel_gather(0, spread)
    left_grad = reduce_end(0, left_copies, left_home, left_own_sum, left_from_sib, left_from_far)
    update(left_in, left_state_in, left_grad, left_out, left_state_out)
    left_all[1, rows_of(near_quarter), :] = left_out[...].astype(bf16)
    left_far, left_sib = left_send(1)
    right_far, right_sib = right_spread(1, rolled)
    table_roll = copy(right_next, right_table.at[1], following)
    state_roll = copy(right_state_next, right_state.at[1], following)
    back = rel_back(0, gathered)
    look_left(1, near_quarter, True)
    left_sib.wait_recv()
    look_left(1, sib_quarter)
    left_far_sib = left_forward(1, left_far)
    rel_update(0, back, rel_in, rel_state_in)
    round_relations(rel_out)
    look_relation(1)
    look_left(1, far_quarter)
    left_far_sib.wait_recv()
    look_left(1, far_sib_quarter)
    look_right(1, near_quarter, True)
    wait_all(right_sib)
    look_right(1, sib_quarter)
    right_far_sib = right_forward(1, right_far)
    look_right(1, far_quarter)
    wait_all(right_far_sib)
    look_right(1, far_sib_quarter)
    dense(1)

    swap = rel_begin(1)
    spread = rel_spread(1, swap)
    right_copies = reduce_begin(
        1, target_at, targets, grad_target, right_to_sib, right_from_sib, right_far_sum, right_own_sum
    )
    right_home = reduce_far(1, right_copies, right_from_sib, right_far_sum, right_to_far, right_from_far)
    left_copies = reduce_begin(
        1, src_at, edges, grad_src, left_to_sib, left_from_sib, left_far_sum, left_own_sum
    )
    left_home = reduce_far(1, left_copies, left_from_sib, left_far_sum, left_to_far, left_from_far)
    gathered = rel_gather(1, spread)
    table_roll.wait_recv()
    state_roll.wait_recv()
    right_grad = reduce_end(1, right_copies, right_home, right_own_sum, right_from_sib, right_from_far)
    update(right_table.at[1], right_state.at[1], right_grad, right_out, right_state_out)
    left_grad = reduce_end(1, left_copies, left_home, left_own_sum, left_from_sib, left_from_far)
    update(left_out, left_state_out, left_grad, left_out, left_state_out)
    back = rel_back(1, gathered)
    rel_update(1, back, rel_out, rel_state_out)
    for made in sent:
        made.wait_send()


def local(
    left_table,
    left_state,
    right_table,
    right_state,
    relations,
    relation_state,
    src_rows,
    dst_rows,
    rel_ids,
    neg_rows,
):
    quarter, width = left_table.shape
    edges = src_rows.shape[1]
    negs = neg_rows.shape[1]
    rels = relations.shape[0]
    slab = quarter * lax.axis_size("edge")
    indices = 3 * edges + negs
    targets = edges + negs
    f32, bf16 = jnp.float32, jnp.bfloat16
    state_shape = (quarter // LANES, LANES)
    rel_state_shape = (rels // LANES, LANES)

    def vmem(shape, kind):
        return pltpu.VMEM(shape, kind)

    results = pl.pallas_call(
        functools.partial(body, lax.axis_size("dom")),
        out_shape=(
            jax.ShapeDtypeStruct((quarter, width), f32),
            jax.ShapeDtypeStruct(state_shape, f32),
            jax.ShapeDtypeStruct((quarter, width), f32),
            jax.ShapeDtypeStruct(state_shape, f32),
            jax.ShapeDtypeStruct((rels, width), f32),
            jax.ShapeDtypeStruct(rel_state_shape, f32),
        ),
        in_specs=[pl.BlockSpec(memory_space=pltpu.VMEM)] * 10,
        out_specs=tuple([pl.BlockSpec(memory_space=pltpu.VMEM)] * 6),
        scratch_shapes=[
            vmem((STEPS, indices, LANES), bf16),
            vmem((STEPS, indices, LANES), bf16),
            vmem((STEPS, 16, indices), bf16),
            vmem((STEPS, LANES, indices), bf16),
            vmem((rels, width), bf16),
            vmem((edges, width), f32),
            vmem((targets, width), f32),
            vmem((edges, width), f32),
            vmem((negs, width), bf16),
            vmem((edges, width), bf16),
            vmem((edges, width), bf16),
            vmem((edges, width), bf16),
            vmem((targets, width), bf16),
            vmem((negs, width), f32),
            vmem((STEPS, slab, width), bf16),
            vmem((STEPS, slab, width), bf16),
            vmem((STEPS, quarter, width), bf16),
            vmem((STEPS, quarter, width), f32),
            vmem((STEPS,) + state_shape, f32),
            vmem((quarter, width), f32),
            vmem(state_shape, f32),
            vmem((quarter, width), f32),
            vmem((quarter, width), f32),
            vmem((quarter, width), f32),
            vmem((quarter, width), f32),
            vmem((rels // 2, width), f32),
            vmem((STEPS, 2, quarter, width), bf16),
            vmem((STEPS, 2, quarter, width), bf16),
            vmem((STEPS, quarter, width), bf16),
            vmem((STEPS, quarter, width), bf16),
            vmem((STEPS, 2, quarter, width), bf16),
            vmem((STEPS, 2, quarter, width), bf16),
            vmem((STEPS, quarter, width), bf16),
            vmem((STEPS, quarter, width), bf16),
            vmem((STEPS, rels // 2, width), bf16),
            vmem((STEPS, rels // 2, width), bf16),
            vmem((STEPS, rels // 2, width), bf16),
            vmem((STEPS, rels // 2, width), bf16),
            vmem((STEPS, rels, width), bf16),
            pltpu.SemaphoreType.DMA((64,)),
            pltpu.SemaphoreType.DMA((64,)),
        ],
        name="buckets",
        compiler_params=pltpu.CompilerParams(
            collective_id=0, has_side_effects=True, vmem_limit_bytes=56 << 20
        ),
    )(
        left_table,
        left_state.reshape(state_shape),
        right_table,
        right_state.reshape(state_shape),
        relations,
        relation_state.reshape(rel_state_shape),
        src_rows,
        dst_rows,
        rel_ids,
        neg_rows,
    )
    left, left_s, right, right_s, rel, rel_s = results
    return (left, left_s.reshape(-1), right, right_s.reshape(-1), rel, rel_s.reshape(-1))


def solution(mesh):
    placed = (
        P(("dom", "edge"), None),
        P(("dom", "edge")),
        P(("dom", "edge"), None),
        P(("dom", "edge")),
        P(),
        P(),
        P(None, ("dom", "edge")),
        P(None, ("dom", "edge")),
        P(None, ("dom", "edge")),
        P(None, ("dom", "edge")),
    )
    return jax.shard_map(
        local,
        mesh=mesh,
        in_specs=placed,
        out_specs=(
            P(("dom", "edge"), None),
            P(("dom", "edge")),
            P(("dom", "edge"), None),
            P(("dom", "edge")),
            P(),
            P(),
        ),
        check_vma=False,
    )
```

time: 596 us -> 138 us (0.23)
  waiting for transfers between devices: 496 us -> 0 us
  Pallas kernels: 0 us -> 130 us
  matrix products: 44.6 us -> 0 us
  other arithmetic: 26.4 us -> 0 us
  between operations: 14.6 us -> 0.66 us
  starting transfers between devices: 6.83 us -> 0 us
    psum x2 -> x0, waiting for transfers between devices: 274 us -> none  [local(): lax.psum(spread_rows(rel_matches, grad_rel), ('dom', 'edge'))]
    reduce_scatter x4 -> x0, waiting for transfers between devices: 138 us -> none  [the longest x2 75.2 us: local(): lax.psum_scatter(scatter_term(target_index, grad_target, quarter * lax.ax...]
    pallas_call x0 -> x1, Pallas kernels: none -> 130 us  [local(): pl.pallas_call(functools.partial(body, lax.axis_size('dom')), out_shape=(...]
    all_gather x4 -> x0, waiting for transfers between devices: 51.4 us -> none  [the longest x2 36.9 us: local(): lax.all_gather(right_b, 'edge', axis=0, tiled=True)]
    dot_general x18 -> x0, matrix products: 44.6 us -> none  [the longest x8 20.5 us: spread_rows(): lax.dot_general(matches, values, (((0,), (0,)), ((), ())), preferred_elem...]
    ppermute x4 -> x0, waiting for transfers between devices: 32.7 us -> none  [passed_along(): return lax.ppermute(value, axis, pairs)]
    reduce_sum x8 -> x0, other arithmetic: 9.37 us -> none  [the longest x6 8.98 us: adagrad(): state = state + jnp.mean(grad * grad, axis=-1)]
    sub x6 -> x0, other arithmetic: 7.63 us -> none  [the longest x4 7.21 us: adagrad(): return (table - learn_rate * grad / jnp.sqrt(state)[:, None], state)]
  transfers between devices with their start and end apart: 14 -> 0, of which waited for: 12 -> 0; matrix products, arithmetic and copies ran while one was open for 8% -> 0% of each run, Pallas kernels for 0% -> 0%
where the time goes in v1:
time: 138 us
  Pallas kernels  130 us (94%)
  local copies, waits for them, and re-layouts  7.63 us (6%)
    pallas_call x1, Pallas kernels, local(): pl.pallas_call(functools.partial(body, lax.axis_size('dom')), out_shape=(...  130 us
    unnamed x12, local copies, waits for them, and re-layouts  7.63 us

profile of v1, /device:TPU:1, one launch (start us, length us, event | category | flops | bytes accessed | tf_op | source)
XLA Modules:
  0.0 138.2 jit_solution(16915430837897361913)
XLA Ops:
  0.6 129.9 %buckets.1 = (f32[512,256]{1,0:T(8,128)}, f32[4,128]{1,0:T(4,128)}, f32[512,256]{1,0:T(8,128)}, f32[4,128]{1,0:T(4,128)}, f32[2048,256]{1,0:T(8,128)}, /*index=5*/f32[16,128]{1,0:T(8,128)}) custom-call(f32[512,256]{1,0:T(8,128)} %left_in.1, f32[4,128]{1,0:T(4,128)} %bitcast.10, f32[512,256]{1,0:T(8,128)} %right_in.1, f32[4,128]{1,0:T(4,128)} %bitcast.11, ...), custom_call_target="tpu_custom_call" | custom-call | tf_op jit(solution)/shard_map/buckets/pallas_call | solution.py:590
  130.6 0.0 copy-start.2
  130.6 0.0 copy-start
  130.6 2.0 %copy.22 = f32[512,256]{1,0:T(8,128)} copy(f32[512,256]{1,0:T(8,128)} %get-tuple-element.24) | data formatting | bytes 1048576
  132.6 1.2 copy.23
  133.8 1.9 %copy.24 = f32[512,256]{1,0:T(8,128)} copy(f32[512,256]{1,0:T(8,128)} %get-tuple-element.26) | data formatting | bytes 1048576
  135.7 0.0 copy-done.2
  135.7 0.6 copy.25
  136.3 0.0 copy-done
  136.3 0.0 copy-start.1
  136.3 1.3 copy.26
  137.6 0.0 copy-done.1
  137.6 0.6 copy.27
Async XLA Ops:
  130.6 5.1 %copy-start.2 = (f32[4,128]{1,0:T(4,128)S(1)}, f32[4,128]{1,0:T(4,128)}, u32[]{:S(2)}) copy-start(f32[4,128]{1,0:T(4,128)} %get-tuple-element.15) | copy-start | bytes 6148
  130.6 5.7 %copy-start = (f32[2048,256]{1,0:T(8,128)S(1)}, f32[2048,256]{1,0:T(8,128)}, u32[]{:S(2)}) copy-start(f32[2048,256]{1,0:T(8,128)} %get-tuple-element.28) | copy-start | bytes 6291460
  136.3 1.3 copy-start.1
